TPU v7x, 32 devices: a whole 2x2x4 slice. The times are simulated.
32 devices in a mesh: band: 4 (over y, x), loc: 8 (over z, core).
Axes of the slice: x: 2, y: 2, z: 4, core: 2. Of those that a mesh axis runs over, the one named last changes fastest.
Arguments:
- tokens: bfloat16 [2048, 16, 768], P('loc', 'band'), may hold values from -6 to 6
- band_index: int32 [16], replicated, may hold values from 0 to 15, each once
- band_table: float32 [16, 768], replicated, may hold values from -3 to 3
- window_ids: int32 [2048], replicated, may hold values from 0 to 1, as said below
- spatial_qkv: bfloat16 [768, 2304], replicated
- spatial_out: bfloat16 [768, 768], replicated, may hold values from -0.21875 to 0.21875
- channel_qkv: bfloat16 [768, 2304], replicated
- channel_out: bfloat16 [768, 768], replicated, may hold values from -0.21875 to 0.21875
- up_weight: bfloat16 [768, 3072], replicated, may hold values from -0.21875 to 0.21875
- down_weight: bfloat16 [3072, 768], replicated, may hold values from -0.109375 to 0.109375
Outputs:
- joined: bfloat16 [2048, 16, 768], P('loc', 'band')
Inputs may be any that keep to these rules, and one draw needn't show every extreme that they name: `window_ids`: each of the 2 windows holds exactly 1024 locations, and each aligned block of 256 locations holds exactly 128 locations of each window. `band_index`: each of the 16 band numbers once.
All inputs are finite; a program needn't handle non-finite values.
Results may differ from a plain program's by a relative error of at most 0.014.
Values may be sent and summed in bfloat16 or wider, within the bound.
No kernel may reach another device: no remote copies, remote signals or barrier semaphores. Data moves between devices by JAX's collectives and lax.ppermute only.
A program may use at most 128 MiB of HBM per device.

v0:
```python
import jax
import jax.numpy as jnp
from jax import lax
from jax.sharding import PartitionSpec as P

HEADS = 12
HEAD_DIM = 64


def norm_rows(values):
    centre = values - jnp.mean(values, axis=-1, keepdims=True)
    spread = jnp.mean(centre * centre, axis=-1, keepdims=True)
    return centre * lax.rsqrt(spread + 1e-05)


def attend(state, query, query_ids, keys, values, key_ids):
    scale = HEAD_DIM ** (-0.5)
    rows, band_dev, width = query.shape
    count = keys.shape[0]
    block = 512
    query_heads = query.reshape(rows, band_dev, HEADS, HEAD_DIM)

    def step(carry, index):
        first = index * block
        key_block = lax.dynamic_slice_in_dim(keys, first, block, 0).reshape(
            block, band_dev, HEADS, HEAD_DIM
        )
        value_block = lax.dynamic_slice_in_dim(values, first, block, 0).reshape(
            block, band_dev, HEADS, HEAD_DIM
        )
        id_block = lax.dynamic_slice_in_dim(key_ids, first, block, 0)
        scores = (
            jnp.einsum(
                "lbhe,pbhe->bhlp", query_heads, key_block, preferred_element_type=jnp.float32
            )
            * scale
        )
        allowed = (query_ids[:, None] == id_block[None, :])[None, None]
        masked = jnp.where(allowed, scores, -1e30)
        peak, total, accum = carry
        new_peak = jnp.maximum(peak, jnp.max(masked, axis=-1))
        expo = jnp.where(allowed, jnp.exp(masked - new_peak[..., None]), 0.0)
        factor = jnp.exp(peak - new_peak)
        total = total * factor + jnp.sum(expo, axis=-1)
        accum = accum * factor[..., None] + jnp.einsum(
            "bhlp,pbhe->bhle",
            expo.astype(jnp.bfloat16),
            value_block,
            preferred_element_type=jnp.float32,
        )
        return ((new_peak, total, accum), None)

    state, unused = lax.scan(step, state, jnp.arange(count // block, dtype=jnp.int32))
    return state


def empty_state(band_dev, loc_dev):
    return (
        jnp.full((band_dev, HEADS, loc_dev), -1e30, jnp.float32),
        jnp.zeros((band_dev, HEADS, loc_dev), jnp.float32),
        jnp.zeros((band_dev, HEADS, loc_dev, HEAD_DIM), jnp.float32),
    )


def heads_result(state, width):
    peak, total, accum = state
    loc_dev = total.shape[2]
    band_dev = total.shape[0]
    return (
        (accum / total[..., None])
        .transpose(2, 0, 1, 3)
        .reshape(loc_dev, band_dev, width)
        .astype(jnp.bfloat16)
    )


def split_qkv(normed, spatial_qkv, loc_dev, band_dev, width):
    packed = jnp.dot(
        normed.reshape(-1, width), spatial_qkv, preferred_element_type=jnp.float32
    ).astype(jnp.bfloat16)
    packed = packed.reshape(loc_dev, band_dev, 3, width)
    return (packed[:, :, 0], packed[:, :, 1], packed[:, :, 2])


def channel_mix(query, keys, values):
    scale = HEAD_DIM ** (-0.5)
    rows, band_query, width = query.shape
    band_keys = keys.shape[1]
    query_heads = query.reshape(rows, band_query, HEADS, HEAD_DIM)
    key_heads = keys.reshape(rows, band_keys, HEADS, HEAD_DIM)
    value_heads = values.reshape(rows, band_keys, HEADS, HEAD_DIM)
    scores = (
        jnp.einsum("rbhe,rche->rhbc", query_heads, key_heads, preferred_element_type=jnp.float32)
        * scale
    )
    peak = jnp.max(scores, axis=-1, keepdims=True)
    expo = jnp.exp(scores - peak)
    total = jnp.sum(expo, axis=-1)
    summed = jnp.einsum(
        "rhbc,rche->rbhe",
        expo.astype(jnp.bfloat16),
        value_heads,
        preferred_element_type=jnp.float32,
    )
    return (
        (summed / jnp.transpose(total, (0, 2, 1))[..., None])
        .astype(jnp.bfloat16)
        .reshape(rows, band_query, width)
    )


def channel_projections(mid, channel_qkv):
    rows, band_count, width = mid.shape
    normed = norm_rows(mid.astype(jnp.float32)).astype(jnp.bfloat16).reshape(-1, width)
    packed = jnp.dot(normed, channel_qkv, preferred_element_type=jnp.float32).astype(jnp.bfloat16)
    packed = packed.reshape(rows, band_count, 3, width)
    return (packed[:, :, 0], packed[:, :, 1], packed[:, :, 2])


def finish(mid, cattn, channel_out, up_weight, down_weight):
    rows, band_count, width = mid.shape
    after = mid.astype(jnp.float32).reshape(-1, width) + jnp.dot(
        cattn.reshape(-1, width), channel_out, preferred_element_type=jnp.float32
    )
    normed = norm_rows(after).astype(jnp.bfloat16)
    hidden = jax.nn.gelu(
        jnp.dot(normed, up_weight, preferred_element_type=jnp.float32), approximate=True
    ).astype(jnp.bfloat16)
    joined = after + jnp.dot(hidden, down_weight, preferred_element_type=jnp.float32)
    return joined.astype(jnp.bfloat16).reshape(rows, band_count, width)


def body(
    tokens,
    band_index,
    band_table,
    window_ids,
    spatial_qkv,
    spatial_out,
    channel_qkv,
    channel_out,
    up_weight,
    down_weight,
):
    loc_dev, band_dev, width = tokens.shape
    band_first = lax.axis_index("band") * band_dev
    mine = lax.dynamic_slice_in_dim(band_index, band_first, band_dev)
    onehot = (mine[:, None] == jnp.arange(band_table.shape[0], dtype=jnp.int32)[None, :]).astype(
        jnp.float32
    )
    embed = jnp.dot(onehot, band_table, precision=lax.Precision.HIGHEST)
    start = tokens.astype(jnp.float32) + embed[None]
    normed = norm_rows(start).astype(jnp.bfloat16)
    my_ids = lax.dynamic_slice_in_dim(window_ids, lax.axis_index("loc") * loc_dev, loc_dev)
    initial = empty_state(band_dev, loc_dev)
    query, keys, values = split_qkv(normed, spatial_qkv, loc_dev, band_dev, width)
    state = attend(
        initial,
        query,
        my_ids,
        lax.all_gather(keys, "loc", axis=0, tiled=True),
        lax.all_gather(values, "loc", axis=0, tiled=True),
        window_ids,
    )
    sattn = heads_result(state, width).reshape(-1, width)
    mid = (
        start.reshape(-1, width) + jnp.dot(sattn, spatial_out, preferred_element_type=jnp.float32)
    ).astype(jnp.bfloat16)
    mid = mid.reshape(loc_dev, band_dev, width)
    groups = lax.axis_size("band")
    blocked = mid.reshape(groups, loc_dev // groups, band_dev, width)
    flat = lax.all_to_all(blocked, "band", split_axis=0, concat_axis=2, tiled=True)[0]
    cquery, ckeys, cvalues = channel_projections(flat, channel_qkv)
    cattn = channel_mix(cquery, ckeys, cvalues)
    mixed = finish(flat, cattn, channel_out, up_weight, down_weight)[None]
    returned = lax.all_to_all(mixed, "band", split_axis=2, concat_axis=0, tiled=True)
    return returned.reshape(loc_dev, band_dev, width)


def solution(mesh):
    placed = (P("loc", "band", None), P(), P(), P(), P(), P(), P(), P(), P(), P())
    return jax.shard_map(
        body, mesh=mesh, in_specs=placed, out_specs=P("loc", "band", None), check_vma=False
    )
```

profile of v0, /device:TPU:0, one launch (start us, length us, event | category | flops | bytes accessed | tf_op | source)
XLA Modules:
  0.0 708.9 jit_solution(8094329962970213311)
XLA Ops:
  20.4 7.4 %convolution_convert_fusion.1 = bf16[1024,2304]{1,0:T(8,128)(2,1)} fusion(bf16[1024,768]{1,0:T(8,128)(2,1)} %reshape.131, bf16[768,2304]{1,0:T(8,128)(2,1)S(1)} %copy-done), kind=kOutput, calls=%fused_computation.34 | convolution fusion | flops 3626237952 | bytes 9830400 | tf_op jit(solution)/shard_map/dot_general | solution.py:78
  27.8 11.3 %reshape.132 = bf16[256,4,3,768]{3,2,1,0:T(4,128)(2,1)} reshape(bf16[1024,2304]{1,0:T(8,128)(2,1)} %convolution_convert_fusion.1) | data formatting | bytes 9437184 | tf_op jit(solution)/shard_map/reshape | solution.py:81
  39.1 13.8 %fusion.58 = (bf16[256,4,1,768]{3,2,1,0:T(2,128)(2,1)S(1)}, bf16[256,4,1,768]{3,2,1,0:T(2,128)(2,1)S(1)}, bf16[256,4,1,768]{3,2,1,0:T(2,128)(2,1)}) fusion(bf16[256,4,3,768]{3,2,1,0:T(4,128)(2,1)} %reshape.132), kind=kLoop, calls=%fused_computation.81 | loop fusion | bytes 9437184 | tf_op jit(solution)/shard_map/slice | solution.py:82
  70.1 104.3 %all-gather.7.cloned.1.call-done = bf16[2048,4,1,768]{3,1,2,0:T(4,128)(2,1)} async-done(((bf16[256,4,1,768]{3,1,2,0:T(4,128)(2,1)}), bf16[2048,4,1,768]{3,1,2,0:T(4,128)(2,1)}) %all-gather.7.cloned.1.call-update) | async-done | bytes 12582928 | tf_op jit(solution)/shard_map/all_gather | solution.py:162
  174.4 116.6 %all-gather.5.cloned.1.call-done = bf16[2048,4,1,768]{3,1,2,0:T(4,128)(2,1)} async-done(((bf16[256,4,1,768]{3,1,2,0:T(4,128)(2,1)}), bf16[2048,4,1,768]{3,1,2,0:T(4,128)(2,1)}) %all-gather.5.cloned.1.call-update) | async-done | bytes 12582928 | tf_op jit(solution)/shard_map/all_gather | solution.py:161
  291.0 229.5 %while.15 = (s32[]{:T(128)}, f32[4,12,256]{2,1,0:T(8,128)S(1)}, f32[4,12,256]{2,1,0:T(8,128)S(1)}, f32[4,12,256,64]{2,3,1,0:T(8,128)}, s32[256]{0:T(256)S(1)}, /...) while((s32[]{:T(128)}, f32[4,12,256]{2,1,0:T(8,128)S(1)}, ...), condition=%wide.region_5.6_spmd.clone, body=%wide.region_2.5_spmd.clone.sunk | while | flops 1694953472 | bytes 153886016 | solution.py:53
  293.2 7.7 %constant_dynamic-slice_fusion.3 = (bf16[512,4,768]{2,1,0:T(4,128)(2,1)}, bf16[512,4,768]{2,1,0:T(4,128)(2,1)}) fusion(bf16[2048,4,768]{2,1,0:T(4,128)(2,1)} %get-tuple-element.281, s32[]{:T(128)S(6)} %select_n.54, bf16[2048,4,768]{2,1,0:T(4,128)(2,1)} %get-tuple-element.279), kind=kLoop, calls=%fused_computation.14.clone.1 | loop fusion | bytes 12582916 | tf_op jit(solution)/shard_map/while/body/eval_jaxpr/dynamic_slice | solution.py:28
  311.1 11.7 %fusion.85 = (f32[4,12,256]{2,1,0:T(8,128)S(1)}, f32[4,12,512,256]{3,2,1,0:T(8,128)}) fusion(pred[256,512]{0,1:T(8,128)(4,1)S(1)} %broadcast_compare_fusion.2, bf16[512,4,12,64]{0,3,2,1:T(8,128)(2,1)S(1)} %bitcast.73, bf16[256,4,12,64]{0,3,2,1:T(8,128)(2,1)} %get-tuple-element.280), kind=kOutput, calls=%fused_computation.2.clone.1 | convolution fusion | flops 824168448 | bytes 30064640 | tf_op jit(solution)/shard_map/while/body/eval_jaxpr/lbhe,pbhe->bhlp/dot_general | solution.py:33
  322.9 12.4 %fusion.86 = f32[4,12,256]{2,1,0:T(8,128)S(1)} fusion(f32[4,12,512,256]{3,2,1,0:T(8,128)} %get-tuple-element.240, f32[4,12,256]{2,1,0:T(8,128)S(1)} %select_maximum_fusion.2, pred[256,512]{0,1:T(8,128)(4,1)S(1)} %broadcast_compare_fusion.2), kind=kLoop, calls=%fused_computation.4.clone.1 | loop fusion | flops 31444992 | bytes 25395200 | tf_op jit(solution)/shard_map/while/body/eval_jaxpr/reduce_sum | solution.py:44
  335.3 11.5 %fusion.88 = f32[4,12,256,64]{2,3,1,0:T(8,128)S(1)} fusion(f32[4,12,256,64]{2,3,1,0:T(8,128)S(1)} %copy-done.6, bf16[512,4,12,64]{0,3,2,1:T(8,128)(2,1)S(1)} %bitcast.74, f32[4,12,512,256]{3,2,1,0:T(8,128)} %get-tuple-element.240, f32[4,12,256]{2,1,0:T(8,128)S(1)} %select_maximum_fusion.2, pred[256,512]{0,1:T(8,128)(4,1)S(1)} %broadcast_compare_fusion.2, ...), kind=kOutput, calls=%fused_computation.8.clone.1 | convolution fusion | flops 839122944 | bytes 34832384 | tf_op jit(solution)/shard_map/while/body/eval_jaxpr/bhlp,pbhe->bhle/dot_general | solution.py:45
  350.6 7.7 %constant_dynamic-slice_fusion.3 = (bf16[512,4,768]{2,1,0:T(4,128)(2,1)}, bf16[512,4,768]{2,1,0:T(4,128)(2,1)}) fusion(bf16[2048,4,768]{2,1,0:T(4,128)(2,1)} %get-tuple-element.281, s32[]{:T(128)S(6)} %select_n.54, bf16[2048,4,768]{2,1,0:T(4,128)(2,1)} %get-tuple-element.279), kind=kLoop, calls=%fused_computation.14.clone.1 | loop fusion | bytes 12582916 | tf_op jit(solution)/shard_map/while/body/eval_jaxpr/dynamic_slice | solution.py:28
  368.5 11.7 %fusion.85 = (f32[4,12,256]{2,1,0:T(8,128)S(1)}, f32[4,12,512,256]{3,2,1,0:T(8,128)}) fusion(pred[256,512]{0,1:T(8,128)(4,1)S(1)} %broadcast_compare_fusion.2, bf16[512,4,12,64]{0,3,2,1:T(8,128)(2,1)S(1)} %bitcast.73, bf16[256,4,12,64]{0,3,2,1:T(8,128)(2,1)} %get-tuple-element.280), kind=kOutput, calls=%fused_computation.2.clone.1 | convolution fusion | flops 824168448 | bytes 30064640 | tf_op jit(solution)/shard_map/while/body/eval_jaxpr/lbhe,pbhe->bhlp/dot_general | solution.py:33
  380.2 12.4 %fusion.86 = f32[4,12,256]{2,1,0:T(8,128)S(1)} fusion(f32[4,12,512,256]{3,2,1,0:T(8,128)} %get-tuple-element.240, f32[4,12,256]{2,1,0:T(8,128)S(1)} %select_maximum_fusion.2, pred[256,512]{0,1:T(8,128)(4,1)S(1)} %broadcast_compare_fusion.2), kind=kLoop, calls=%fused_computation.4.clone.1 | loop fusion | flops 31444992 | bytes 25395200 | tf_op jit(solution)/shard_map/while/body/eval_jaxpr/reduce_sum | solution.py:44
  392.7 11.5 %fusion.88 = f32[4,12,256,64]{2,3,1,0:T(8,128)S(1)} fusion(f32[4,12,256,64]{2,3,1,0:T(8,128)S(1)} %copy-done.6, bf16[512,4,12,64]{0,3,2,1:T(8,128)(2,1)S(1)} %bitcast.74, f32[4,12,512,256]{3,2,1,0:T(8,128)} %get-tuple-element.240, f32[4,12,256]{2,1,0:T(8,128)S(1)} %select_maximum_fusion.2, pred[256,512]{0,1:T(8,128)(4,1)S(1)} %broadcast_compare_fusion.2, ...), kind=kOutput, calls=%fused_computation.8.clone.1 | convolution fusion | flops 839122944 | bytes 34832384 | tf_op jit(solution)/shard_map/while/body/eval_jaxpr/bhlp,pbhe->bhle/dot_general | solution.py:45
  407.9 7.7 %constant_dynamic-slice_fusion.3 = (bf16[512,4,768]{2,1,0:T(4,128)(2,1)}, bf16[512,4,768]{2,1,0:T(4,128)(2,1)}) fusion(bf16[2048,4,768]{2,1,0:T(4,128)(2,1)} %get-tuple-element.281, s32[]{:T(128)S(6)} %select_n.54, bf16[2048,4,768]{2,1,0:T(4,128)(2,1)} %get-tuple-element.279), kind=kLoop, calls=%fused_computation.14.clone.1 | loop fusion | bytes 12582916 | tf_op jit(solution)/shard_map/while/body/eval_jaxpr/dynamic_slice | solution.py:28
  425.8 11.7 %fusion.85 = (f32[4,12,256]{2,1,0:T(8,128)S(1)}, f32[4,12,512,256]{3,2,1,0:T(8,128)}) fusion(pred[256,512]{0,1:T(8,128)(4,1)S(1)} %broadcast_compare_fusion.2, bf16[512,4,12,64]{0,3,2,1:T(8,128)(2,1)S(1)} %bitcast.73, bf16[256,4,12,64]{0,3,2,1:T(8,128)(2,1)} %get-tuple-element.280), kind=kOutput, calls=%fused_computation.2.clone.1 | convolution fusion | flops 824168448 | bytes 30064640 | tf_op jit(solution)/shard_map/while/body/eval_jaxpr/lbhe,pbhe->bhlp/dot_general | solution.py:33
  437.6 12.4 %fusion.86 = f32[4,12,256]{2,1,0:T(8,128)S(1)} fusion(f32[4,12,512,256]{3,2,1,0:T(8,128)} %get-tuple-element.240, f32[4,12,256]{2,1,0:T(8,128)S(1)} %select_maximum_fusion.2, pred[256,512]{0,1:T(8,128)(4,1)S(1)} %broadcast_compare_fusion.2), kind=kLoop, calls=%fused_computation.4.clone.1 | loop fusion | flops 31444992 | bytes 25395200 | tf_op jit(solution)/shard_map/while/body/eval_jaxpr/reduce_sum | solution.py:44
  450.1 11.5 %fusion.88 = f32[4,12,256,64]{2,3,1,0:T(8,128)S(1)} fusion(f32[4,12,256,64]{2,3,1,0:T(8,128)S(1)} %copy-done.6, bf16[512,4,12,64]{0,3,2,1:T(8,128)(2,1)S(1)} %bitcast.74, f32[4,12,512,256]{3,2,1,0:T(8,128)} %get-tuple-element.240, f32[4,12,256]{2,1,0:T(8,128)S(1)} %select_maximum_fusion.2, pred[256,512]{0,1:T(8,128)(4,1)S(1)} %broadcast_compare_fusion.2, ...), kind=kOutput, calls=%fused_computation.8.clone.1 | convolution fusion | flops 839122944 | bytes 34832384 | tf_op jit(solution)/shard_map/while/body/eval_jaxpr/bhlp,pbhe->bhle/dot_general | solution.py:45
  465.3 7.7 %constant_dynamic-slice_fusion.3 = (bf16[512,4,768]{2,1,0:T(4,128)(2,1)}, bf16[512,4,768]{2,1,0:T(4,128)(2,1)}) fusion(bf16[2048,4,768]{2,1,0:T(4,128)(2,1)} %get-tuple-element.281, s32[]{:T(128)S(6)} %select_n.54, bf16[2048,4,768]{2,1,0:T(4,128)(2,1)} %get-tuple-element.279), kind=kLoop, calls=%fused_computation.14.clone.1 | loop fusion | bytes 12582916 | tf_op jit(solution)/shard_map/while/body/eval_jaxpr/dynamic_slice | solution.py:28
  483.2 11.7 %fusion.85 = (f32[4,12,256]{2,1,0:T(8,128)S(1)}, f32[4,12,512,256]{3,2,1,0:T(8,128)}) fusion(pred[256,512]{0,1:T(8,128)(4,1)S(1)} %broadcast_compare_fusion.2, bf16[512,4,12,64]{0,3,2,1:T(8,128)(2,1)S(1)} %bitcast.73, bf16[256,4,12,64]{0,3,2,1:T(8,128)(2,1)} %get-tuple-element.280), kind=kOutput, calls=%fused_computation.2.clone.1 | convolution fusion | flops 824168448 | bytes 30064640 | tf_op jit(solution)/shard_map/while/body/eval_jaxpr/lbhe,pbhe->bhlp/dot_general | solution.py:33
  495.0 12.4 %fusion.86 = f32[4,12,256]{2,1,0:T(8,128)S(1)} fusion(f32[4,12,512,256]{3,2,1,0:T(8,128)} %get-tuple-element.240, f32[4,12,256]{2,1,0:T(8,128)S(1)} %select_maximum_fusion.2, pred[256,512]{0,1:T(8,128)(4,1)S(1)} %broadcast_compare_fusion.2), kind=kLoop, calls=%fused_computation.4.clone.1 | loop fusion | flops 31444992 | bytes 25395200 | tf_op jit(solution)/shard_map/while/body/eval_jaxpr/reduce_sum | solution.py:44
  507.5 11.5 %fusion.88 = f32[4,12,256,64]{2,3,1,0:T(8,128)S(1)} fusion(f32[4,12,256,64]{2,3,1,0:T(8,128)S(1)} %copy-done.6, bf16[512,4,12,64]{0,3,2,1:T(8,128)(2,1)S(1)} %bitcast.74, f32[4,12,512,256]{3,2,1,0:T(8,128)} %get-tuple-element.240, f32[4,12,256]{2,1,0:T(8,128)S(1)} %select_maximum_fusion.2, pred[256,512]{0,1:T(8,128)(4,1)S(1)} %broadcast_compare_fusion.2, ...), kind=kOutput, calls=%fused_computation.8.clone.1 | convolution fusion | flops 839122944 | bytes 34832384 | tf_op jit(solution)/shard_map/while/body/eval_jaxpr/bhlp,pbhe->bhle/dot_general | solution.py:45
  522.9 6.7 copy.73
  529.6 6.2 convert_element_type.74
  543.0 24.0 %all_to_all.24 = bf16[4,64,4,768]{3,2,1,0:T(4,128)(2,1)S(1)} all-to-all(bf16[4,64,4,768]{3,2,1,0:T(4,128)(2,1)S(1)} %reshape_reshape.6), channel_id=1, replica_groups=mesh['band'=4,'loc'=8] {'band'}, dimensions={0} | all-to-all | bytes 3145728 | tf_op jit(solution)/shard_map/all_to_all | solution.py:172
  573.3 9.1 %convolution_convert_fusion = bf16[1024,2304]{1,0:T(8,128)(2,1)} fusion(bf16[768,2304]{1,0:T(8,128)(2,1)} %param.18, f32[1024,768]{1,0:T(8,128)} %reshape.135, f32[1024]{0:T(1024)S(1)} %rsqrt.29, f32[1024]{0:T(1024)S(1)} %div.41), kind=kOutput, calls=%fused_computation.33 | convolution fusion | flops 3628597248 | bytes 11411456 | tf_op jit(solution)/shard_map/dot_general | solution.py:115
  582.4 11.3 %reshape.133 = bf16[64,16,3,768]{3,2,1,0:T(4,128)(2,1)} reshape(bf16[1024,2304]{1,0:T(8,128)(2,1)} %convolution_convert_fusion) | data formatting | bytes 9437184 | tf_op jit(solution)/shard_map/reshape | solution.py:116
  593.7 24.9 %slice_reduce_fusion.2 = (bf16[64,16,768]{2,1,0:T(8,128)(2,1)}, bf16[64,16,768]{2,1,0:T(8,128)(2,1)S(1)}, bf16[64,16,768]{2,1,0:T(8,128)(2,1)S(1)}) fusion(bf16[64,16,3,768]{3,2,1,0:T(4,128)(2,1)} %reshape.133), kind=kLoop, calls=%fused_computation.40 | loop fusion | bytes 9437184 | tf_op jit(solution)/shard_map/slice | solution.py:117
  618.6 6.0 reshape_squeeze.13
  647.7 6.2 reshape_reshape.7
  659.4 16.6 %add_convert_fusion = bf16[1024,768]{1,0:T(8,128)(2,1)} fusion(f32[1024,768]{1,0:T(8,128)} %copy-done.9, bf16[3072,768]{1,0:T(8,128)(2,1)} %param.21, bf16[768,3072]{1,0:T(8,128)(2,1)} %param.20, f32[1024]{0:T(1024)S(1)} %add_rsqrt_fusion.2, f32[1024]{0:T(1024)S(1)} %broadcast_multiply_fusion.2), kind=kOutput, calls=%fused_computation.46 | convolution fusion | flops 9695920128 | bytes 14163968 | tf_op jit(solution)/shard_map/dot_general | solution.py:129
  678.1 21.4 %all_to_all.25 = bf16[1,64,16,768]{3,1,0,2:T(8,128)(2,1)S(1)} all-to-all(bf16[1,64,16,768]{3,1,0,2:T(8,128)(2,1)S(1)} %copy.85), channel_id=1, replica_groups=mesh['band'=4,'loc'=8] {'band'}, dimensions={2} | all-to-all | bytes 3145728 | tf_op jit(solution)/shard_map/all_to_all | solution.py:176
  (117 shorter events, 133.2 us)
Async XLA Ops:
  6.5 13.9 %copy-start = (bf16[768,2304]{1,0:T(8,128)(2,1)S(1)}, bf16[768,2304]{1,0:T(8,128)(2,1)}, u32[]{:S(2)}) copy-start(bf16[768,2304]{1,0:T(8,128)(2,1)} %param.16) | copy-start | bytes 10616836
  6.5 167.9 %all-gather.7.cloned.1.call-start = ((), (), s32[]{:S(2)}) async-start(), calls=%async_computation.3 | async-start | bytes 14155776 | tf_op jit(solution)/shard_map/all_gather | solution.py:162
  6.5 7.3 %copy-start.3 = (bf16[256,4,768]{2,1,0:T(4,128)(2,1)S(1)}, bf16[256,4,768]{2,1,0:T(4,128)(2,1)}, u32[]{:S(2)}) copy-start(bf16[256,4,768]{2,1,0:T(4,128)(2,1)} %param.12) | copy-start | bytes 4718596
  54.8 236.2 %all-gather.5.cloned.1.call-start = ((), (), s32[]{:S(2)}) async-start(), calls=%async_computation.2 | async-start | bytes 14155776 | tf_op jit(solution)/shard_map/all_gather | solution.py:161
  322.8 12.5 %copy-start.2 = (bf16[512,4,768]{0,2,1:T(8,128)(2,1)S(1)}, bf16[512,4,768]{0,2,1:T(8,128)(2,1)}, u32[]{:S(2)}) copy-start(bf16[512,4,768]{0,2,1:T(8,128)(2,1)} %copy.114) | copy-start | bytes 9437188 | tf_op jit(solution)/shard_map/while
  322.9 12.5 %copy-start.6 = (f32[4,12,256,64]{2,3,1,0:T(8,128)S(1)}, f32[4,12,256,64]{2,3,1,0:T(8,128)}, u32[]{:S(2)}) copy-start(f32[4,12,256,64]{2,3,1,0:T(8,128)} %get-tuple-element.261) | copy-start | bytes 9437188 | tf_op jit(solution)/shard_map/while
  346.8 1.6 copy-start.7
  380.2 12.5 %copy-start.2 = (bf16[512,4,768]{0,2,1:T(8,128)(2,1)S(1)}, bf16[512,4,768]{0,2,1:T(8,128)(2,1)}, u32[]{:S(2)}) copy-start(bf16[512,4,768]{0,2,1:T(8,128)(2,1)} %copy.114) | copy-start | bytes 9437188 | tf_op jit(solution)/shard_map/while
  380.2 12.5 %copy-start.6 = (f32[4,12,256,64]{2,3,1,0:T(8,128)S(1)}, f32[4,12,256,64]{2,3,1,0:T(8,128)}, u32[]{:S(2)}) copy-start(f32[4,12,256,64]{2,3,1,0:T(8,128)} %get-tuple-element.261) | copy-start | bytes 9437188 | tf_op jit(solution)/shard_map/while
  404.2 1.6 copy-start.7
  437.6 12.5 %copy-start.2 = (bf16[512,4,768]{0,2,1:T(8,128)(2,1)S(1)}, bf16[512,4,768]{0,2,1:T(8,128)(2,1)}, u32[]{:S(2)}) copy-start(bf16[512,4,768]{0,2,1:T(8,128)(2,1)} %copy.114) | copy-start | bytes 9437188 | tf_op jit(solution)/shard_map/while
  437.6 12.5 %copy-start.6 = (f32[4,12,256,64]{2,3,1,0:T(8,128)S(1)}, f32[4,12,256,64]{2,3,1,0:T(8,128)}, u32[]{:S(2)}) copy-start(f32[4,12,256,64]{2,3,1,0:T(8,128)} %get-tuple-element.261) | copy-start | bytes 9437188 | tf_op jit(solution)/shard_map/while
  461.5 1.6 copy-start.7
  495.0 12.5 %copy-start.2 = (bf16[512,4,768]{0,2,1:T(8,128)(2,1)S(1)}, bf16[512,4,768]{0,2,1:T(8,128)(2,1)}, u32[]{:S(2)}) copy-start(bf16[512,4,768]{0,2,1:T(8,128)(2,1)} %copy.114) | copy-start | bytes 9437188 | tf_op jit(solution)/shard_map/while
  495.0 12.5 %copy-start.6 = (f32[4,12,256,64]{2,3,1,0:T(8,128)S(1)}, f32[4,12,256,64]{2,3,1,0:T(8,128)}, u32[]{:S(2)}) copy-start(f32[4,12,256,64]{2,3,1,0:T(8,128)} %get-tuple-element.261) | copy-start | bytes 9437188 | tf_op jit(solution)/shard_map/while
  518.9 1.6 copy-start.7
  529.6 6.2 copy-start.5
  638.0 2.3 copy-start.4
  647.7 6.2 copy-start.8
  657.2 1.7 copy-start.9
  676.1 25.8 %copy-start.1 = (bf16[768,2304]{1,0:T(8,128)(2,1)S(1)}, bf16[768,2304]{1,0:T(8,128)(2,1)}, u32[]{:S(2)}) copy-start(bf16[768,2304]{1,0:T(8,128)(2,1)} %param.16) | copy-start | bytes 10616836
Sparse Core Ops, SparseCore 0:
  54.9 119.4 all-gather.6
  176.0 114.9 all-gather.4
where the time goes:
time: 718 us; the launch traced here: 709 us
  waiting for transfers between devices  221 us (31%)
  local copies, waits for them, and re-layouts  215 us (30%)
  matrix products  145 us (20%)
  other arithmetic  66 us (9%)
  blocking collectives  45.4 us (6%)
  between operations  13.8 us (2%)
    all_gather x1, waiting for transfers between devices, body(): lax.all_gather(keys, 'loc', axis=0, tiled=True)  117 us
    all_gather x1, waiting for transfers between devices, body(): lax.all_gather(values, 'loc', axis=0, tiled=True)  104 us
    dynamic_slice x8, local copies, waits for them, and re-layouts, step(): lax.dynamic_slice_in_dim(values, first, block, 0)  54.3 us
    reduce_sum x4, other arithmetic, step(): total = total * factor + jnp.sum(expo, axis=-1)  49.5 us
    dot_general x4, matrix products, step(): jnp.einsum('lbhe,pbhe->bhlp', query_heads, key_block, preferred_element_t...  47 us
    dot_general x4, matrix products, step(): jnp.einsum('bhlp,pbhe->bhle', expo.astype(jnp.bfloat16), value_block, pre...  45.8 us
    slice x4, local copies, waits for them, and re-layouts, split_qkv(): return (packed[:, :, 0], packed[:, :, 1], packed[:, :, 2])  25 us
    slice x1, local copies, waits for them, and re-layouts, channel_projections(): return (packed[:, :, 0], packed[:, :, 1], packed[:, :, 2])  24.9 us
  transfers between devices with their start and end apart: 2, of which 2 were waited for; matrix products, arithmetic and copies ran while one was open for 2% of the time, Pallas kernels for 0%

commit v1 on v0

v1 whole, which is shorter than its diff:
```python
import functools

import jax
import jax.numpy as jnp
from jax import lax
from jax.experimental import pallas as pl
from jax.experimental.pallas import tpu as pltpu
from jax.sharding import PartitionSpec as P

HEADS = 12
HEAD_DIM = 64
WINDOWS = 2
CHUNKS = 2
LATE_SLOTS = 2
TILE_LOCS = 16
LANES = 128
QUERY_SCALE = HEAD_DIM ** (-0.5) * 1.4426950408889634
VMEM_LIMIT = 56 * 1024 * 1024

F32 = jnp.float32
BF16 = jnp.bfloat16


def dot(left, right):
    return jnp.dot(left, right, preferred_element_type=F32)


def dot_t(left, right):
    return lax.dot_general(left, right, (((1,), (1,)), ((), ())), preferred_element_type=F32)


def norm_rows(values):
    centre = values - jnp.mean(values, axis=-1, keepdims=True)
    spread = jnp.mean(centre * centre, axis=-1, keepdims=True)
    return centre * lax.rsqrt(spread + 1e-05)


def call(kernel, out_shape, flops, nbytes, **kwargs):
    return pl.pallas_call(
        kernel,
        out_shape=out_shape,
        compiler_params=pltpu.CompilerParams(vmem_limit_bytes=VMEM_LIMIT),
        cost_estimate=pl.CostEstimate(flops=flops, bytes_accessed=nbytes, transcendentals=0),
        **kwargs,
    )


def exchange(value, axis, step):
    if step == 0:
        return value
    return lax.ppermute(value, axis, [(i, i ^ step) for i in range(lax.axis_size(axis))])


class Plan:
    def __init__(self, tokens):
        self.loc_dev, self.band_dev, self.width = tokens.shape
        self.locs = lax.axis_size("loc")
        self.groups = lax.axis_size("band")
        self.share = self.locs // (self.band_dev * WINDOWS)
        assert self.share * self.band_dev * WINDOWS == self.locs
        self.block = self.loc_dev // WINDOWS
        self.rows = self.block // self.share
        self.chunks = CHUNKS
        self.chunk_rows = self.rows // self.chunks
        self.part_rows = self.chunk_rows // self.groups
        assert self.part_rows * self.groups * self.chunks * self.share == self.block


def location_keys(plan, ids):
    size = plan.loc_dev
    row = jnp.broadcast_to(ids.astype(F32), (size, size))
    first = lax.broadcasted_iota(jnp.int32, (size, size), 0)
    second = lax.broadcasted_iota(jnp.int32, (size, size), 1)
    column = jnp.sum(jnp.where(first == second, row, 0.0), axis=1, keepdims=True)
    before = jnp.where((column == row) & (first < second), 1.0, 0.0)
    rank = jnp.sum(before, axis=0, keepdims=True)
    return ids.astype(F32) * plan.block + rank


def arrange(plan, tokens, ids):
    def kernel(ids_ref, x_ref, *rest):
        outs, bands = rest[: plan.locs], rest[plan.locs]
        me = lax.axis_index("loc")
        group = lax.axis_index("band")
        keys = location_keys(plan, ids_ref[pl.ds(me, 1), :])
        for band in range(plan.band_dev):
            bands[band] = x_ref[:, band, :]
        place = lax.broadcasted_iota(jnp.int32, (plan.rows, plan.loc_dev), 0)
        chunk = place // plan.chunk_rows
        owner = (place // plan.part_rows) % plan.groups
        rank = chunk * plan.chunk_rows + (owner ^ group) * plan.part_rows + place % plan.part_rows
        for slot in range(plan.locs):
            peer = me ^ slot
            window = peer % WINDOWS
            part = (peer // WINDOWS) % plan.share
            band = peer // (WINDOWS * plan.share)
            wanted = rank + (window * plan.block + part * plan.rows)
            pick = jnp.where(wanted.astype(F32) == keys, 1.0, 0.0).astype(BF16)
            outs[slot][...] = dot(pick, bands[band]).astype(BF16)

    shape = jax.ShapeDtypeStruct((plan.rows, plan.width), BF16)
    return call(
        kernel,
        [shape] * plan.locs,
        2 * plan.loc_dev * tokens.size,
        4 * tokens.size,
        scratch_shapes=[pltpu.VMEM((plan.band_dev, plan.loc_dev, plan.width), BF16)],
    )(ids, tokens)


def embed_row(plan, index_ref, table_ref):
    band = lax.axis_index("loc") // (WINDOWS * plan.share)
    number = index_ref[lax.axis_index("band") * plan.band_dev + band]
    return table_ref[pl.ds(number, 1), :]


SMEM = pl.BlockSpec(memory_space=pltpu.SMEM)
VMEM = pl.BlockSpec(memory_space=pltpu.VMEM)


def project(plan, slots, index, table, weights):
    count = len(slots)
    width = plan.width

    def kernel(index_ref, table_ref, w_ref, *rest):
        ins, (q_ref, k_ref, v_ref) = rest[:count], rest[count:]
        embed = embed_row(plan, index_ref, table_ref)
        for first in range(0, count, 2):
            some = ins[first : first + 2]
            rows = jnp.concatenate([ref[...].astype(F32) for ref in some], axis=0) + embed
            normed = norm_rows(rows).astype(BF16)
            here = pl.ds(first * plan.rows, len(some) * plan.rows)
            q_ref[here, :] = (dot(normed, w_ref[:, :width]) * QUERY_SCALE).astype(BF16)
            k_ref[here, :] = dot(normed, w_ref[:, width : 2 * width]).astype(BF16)
            v_ref[here, :] = dot(normed, w_ref[:, 2 * width :]).astype(BF16)

    rows = count * plan.rows
    shape = jax.ShapeDtypeStruct((rows, width), BF16)
    return call(
        kernel,
        [shape] * 3,
        2 * rows * width * 3 * width,
        2 * (4 * rows * width + 3 * width * width),
        in_specs=[SMEM, VMEM, VMEM] + [VMEM] * count,
    )(index, table, weights, *slots)


def head_sums(scores, values, ones):
    peak = functools.reduce(
        jnp.maximum, [jnp.max(piece, axis=-1, keepdims=True) for piece in scores]
    )
    total = None
    for piece, value in zip(scores, values):
        part = dot(
            jnp.exp2(piece - peak).astype(BF16), jnp.concatenate([value, ones(value)], axis=1)
        )
        total = part if total is None else total + part
    return total[:, :LANES] / total[:, LANES:]


def ones_like_block(value):
    return jnp.ones(value.shape, BF16)


def pair_attention(query, keys, values, mask=None):
    lane = lax.broadcasted_iota(jnp.int32, query.shape, 1)
    result = None
    for head in range(LANES // HEAD_DIM):
        inside = (lane // HEAD_DIM) == head
        only = jnp.where(inside, query, jnp.zeros_like(query))
        scores = [dot_t(only, piece) for piece in keys]
        if mask is not None:
            scores = [jnp.where(mask, piece, -1e30) for piece in scores]
        mine = head_sums(scores, values, ones_like_block)
        result = mine if result is None else jnp.where(inside, mine, result)
    return result.astype(BF16)


def attend(plan, chunk, query, keys, values, slots, index, table, spatial_out):
    width, rows = plan.width, plan.chunk_rows
    pieces, sources = len(keys), len(query)
    counts = [piece.shape[0] // plan.rows for piece in query]
    total = plan.locs * rows
    pairs = width // LANES

    def kernel(index_ref, table_ref, w_ref, *rest):
        q_refs, rest = rest[:sources], rest[sources:]
        k_refs, rest = rest[:pieces], rest[pieces:]
        v_refs, rest = rest[:pieces], rest[pieces:]
        slot_refs, rest = rest[: plan.locs], rest[plan.locs :]
        outs, result = rest[: plan.locs], rest[plan.locs]
        pair = pl.program_id(0)
        query_rows = jnp.concatenate(
            [ref[...].reshape(count * rows, LANES) for ref, count in zip(q_refs, counts)], axis=0
        )
        result[pair] = pair_attention(
            query_rows, [ref[...] for ref in k_refs], [ref[...] for ref in v_refs]
        )

        @pl.when(pair == pairs - 1)
        def _():
            embed = embed_row(plan, index_ref, table_ref)
            attended = jnp.concatenate([result[i] for i in range(pairs)], axis=1)
            added = dot(attended, w_ref[...])
            for slot in range(plan.locs):
                start = slot_refs[slot][...].astype(F32) + embed
                outs[slot][...] = (start + added[slot * rows : (slot + 1) * rows]).astype(BF16)

    q_specs = [pl.BlockSpec((count, rows, LANES), lambda p: (0, chunk, p)) for count in counts]
    kv_specs = [pl.BlockSpec((piece.shape[0], LANES), lambda p: (0, p)) for piece in keys]
    slot_specs = [pl.BlockSpec((rows, width), lambda p: (chunk, 0))] * plan.locs
    out_specs = [pl.BlockSpec((rows, width), lambda p: (0, 0))] * plan.locs
    key_rows = sum(piece.shape[0] for piece in keys)
    return call(
        kernel,
        [jax.ShapeDtypeStruct((rows, width), BF16)] * plan.locs,
        16 * total * key_rows * width,
        2 * width * (2 * key_rows + 3 * total + width),
        grid=(pairs,),
        in_specs=[SMEM, VMEM, VMEM] + q_specs + kv_specs + kv_specs + slot_specs,
        out_specs=out_specs,
        scratch_shapes=[pltpu.VMEM((pairs, total, LANES), BF16)],
    )(
        index,
        table,
        spatial_out,
        *[piece.reshape(count, plan.rows, width) for piece, count in zip(query, counts)],
        *keys,
        *values,
        *slots,
    )


def regroup(plan, slots):
    rows = plan.part_rows
    if rows % 16:
        stacked = jnp.stack(slots).reshape(plan.locs, plan.groups, rows, plan.width)
        return [stacked[:, owner] for owner in range(plan.groups)]

    def kernel(*refs):
        ins, outs, sems = refs[: plan.locs], refs[plan.locs : -1], refs[-1]
        copies = [
            pltpu.make_async_copy(
                ins[slot].at[pl.ds(owner * rows, rows), :],
                outs[owner].at[slot],
                sems.at[slot * plan.groups + owner],
            )
            for slot in range(plan.locs)
            for owner in range(plan.groups)
        ]
        for copy in copies:
            copy.start()
        for copy in copies:
            copy.wait()

    shape = jax.ShapeDtypeStruct((plan.locs, rows, plan.width), BF16)
    anywhere = pl.BlockSpec(memory_space=pl.ANY)
    return call(
        kernel,
        [shape] * plan.groups,
        0,
        4 * plan.locs * plan.chunk_rows * plan.width,
        in_specs=[anywhere] * plan.locs,
        out_specs=[anywhere] * plan.groups,
        scratch_shapes=[pltpu.SemaphoreType.DMA((plan.locs * plan.groups,))],
    )(*slots)


def channel(plan, parts, channel_qkv, channel_out, up_weight, down_weight):
    groups, width = plan.groups, plan.width
    bands, locations, _ = parts[0].shape
    tile = TILE_LOCS
    assert locations % tile == 0
    rows = groups * bands * tile

    def kernel(qkv_ref, out_ref, up_ref, down_ref, *refs):
        ins, outs = refs[:groups], refs[groups:]
        mid = jnp.concatenate(
            [ref[...].reshape(bands * tile, width) for ref in ins], axis=0
        ).astype(F32)
        normed = norm_rows(mid).astype(BF16)
        query = (dot(normed, qkv_ref[:, :width]) * QUERY_SCALE).astype(BF16)
        keys = dot(normed, qkv_ref[:, width : 2 * width]).astype(BF16)
        values = dot(normed, qkv_ref[:, 2 * width :]).astype(BF16)
        first = lax.broadcasted_iota(jnp.int32, (rows, rows), 0)
        second = lax.broadcasted_iota(jnp.int32, (rows, rows), 1)
        mask = (first % tile) == (second % tile)
        attended = []
        for pair in range(width // LANES):
            here = slice(pair * LANES, (pair + 1) * LANES)
            attended.append(
                pair_attention(query[:, here], [keys[:, here]], [values[:, here]], mask)
            )
        after = mid + dot(jnp.concatenate(attended, axis=1), out_ref[...])
        normed = norm_rows(after).astype(BF16)
        hidden = jax.nn.gelu(dot(normed, up_ref[...]), approximate=True).astype(BF16)
        joined = (after + dot(hidden, down_ref[...])).astype(BF16)
        for owner in range(groups):
            outs[owner][...] = joined[owner * bands * tile : (owner + 1) * bands * tile].reshape(
                bands, tile, width
            )

    block = pl.BlockSpec((bands, tile, width), lambda i: (0, i, 0))
    weights = channel_qkv.size + channel_out.size + up_weight.size + down_weight.size
    count = groups * bands * locations
    return call(
        kernel,
        [jax.ShapeDtypeStruct((bands, locations, width), BF16)] * groups,
        2 * count * weights,
        2 * (2 * count * width + weights),
        grid=(locations // tile,),
        in_specs=[VMEM] * 4 + [block] * groups,
        out_specs=[block] * groups,
    )(channel_qkv, channel_out, up_weight, down_weight, *parts)


def restore(plan, ids, returned):
    locations = plan.loc_dev // (plan.chunks * plan.groups)

    def kernel(ids_ref, *refs):
        ins, out_ref = refs[:-1], refs[-1]
        me = lax.axis_index("loc")
        group = lax.axis_index("band")
        keys = location_keys(plan, ids_ref[pl.ds(me, 1), :])
        place = lax.broadcasted_iota(jnp.int32, (plan.loc_dev, plan.loc_dev), 0)
        inner = place % plan.part_rows
        window = (place // plan.part_rows) % WINDOWS ^ (me % WINDOWS)
        part = (place // (plan.part_rows * WINDOWS)) % plan.share ^ (me // WINDOWS) % plan.share
        owner = (place // locations) % plan.groups ^ group
        chunk = place // (locations * plan.groups)
        wanted = (
            window * plan.block
            + part * plan.rows
            + chunk * plan.chunk_rows
            + owner * plan.part_rows
            + inner
        )
        pick = jnp.where(wanted.astype(F32) == keys, 1.0, 0.0).astype(BF16)
        mine = me // (WINDOWS * plan.share)
        for band in range(plan.band_dev):
            rows = jnp.concatenate([ref[band ^ mine] for ref in ins], axis=0)
            out_ref[:, band, :] = lax.dot_general(
                pick, rows, (((0,), (0,)), ((), ())), preferred_element_type=F32
            ).astype(BF16)

    arrays = [array for chunk in returned for array in chunk]
    size = plan.loc_dev * plan.band_dev * plan.width
    return call(
        kernel,
        jax.ShapeDtypeStruct((plan.loc_dev, plan.band_dev, plan.width), BF16),
        2 * plan.loc_dev * size,
        4 * size,
    )(ids, *arrays)


def body(
    tokens,
    band_index,
    band_table,
    window_ids,
    spatial_qkv,
    spatial_out,
    channel_qkv,
    channel_out,
    up_weight,
    down_weight,
):
    plan = Plan(tokens)
    ids = window_ids.reshape(plan.locs, plan.loc_dev)
    sent = arrange(plan, tokens, ids)
    slots = [exchange(value, "loc", step) for step, value in enumerate(sent)]
    split = plan.locs - LATE_SLOTS
    early = project(plan, slots[:split], band_index, band_table, spatial_qkv)
    late = project(plan, slots[split:], band_index, band_table, spatial_qkv)
    query, keys, values = zip(early, late)
    if plan.share > 1:
        same = [
            [(band * plan.share + part) * WINDOWS + window for part in range(plan.share)]
            for band in range(plan.band_dev)
            for window in range(WINDOWS)
        ]
        gather = functools.partial(
            lax.all_gather, axis_name="loc", axis_index_groups=same, axis=0, tiled=True
        )
        keys = [gather(jnp.concatenate(keys, axis=0))]
        values = [gather(jnp.concatenate(values, axis=0))]
    returned = []
    for chunk in range(plan.chunks):
        mid = attend(
            plan, chunk, query, keys, values, slots, band_index, band_table, spatial_out
        )
        back = [exchange(value, "loc", step) for step, value in enumerate(mid)]
        parts = regroup(plan, back)
        parts = [exchange(value, "band", step) for step, value in enumerate(parts)]
        parts = [part.reshape(plan.band_dev, -1, plan.width) for part in parts]
        done = channel(plan, parts, channel_qkv, channel_out, up_weight, down_weight)
        returned.append([exchange(value, "band", step) for step, value in enumerate(done)])
    return restore(plan, ids, returned)


def solution(mesh):
    placed = (P("loc", "band", None), P(), P(), P(), P(), P(), P(), P(), P(), P())
    return jax.shard_map(
        body, mesh=mesh, in_specs=placed, out_specs=P("loc", "band", None), check_vma=False
    )
```

time: 718 us -> 224 us (0.31); the launches traced: 709 us -> 224 us
  local copies, waits for them, and re-layouts: 215 us -> 4.88 us
  waiting for transfers between devices: 221 us -> 26.1 us
  matrix products: 145 us -> 0 us
  Pallas kernels: 0 us -> 141 us
  other arithmetic: 66 us -> 0 us
  starting transfers between devices: 0.22 us -> 51.4 us
  blocking collectives: 45.4 us -> 0 us
  between operations: 13.8 us -> 0.31 us
    all_gather x2 -> x0, waiting for transfers between devices: 221 us -> none  [the longest x1 117 us: body(): lax.all_gather(keys, 'loc', axis=0, tiled=True)]
    dot_general x16 -> x0, matrix products: 145 us -> none  [the longest x4 47 us: step(): jnp.einsum('lbhe,pbhe->bhlp', query_heads, key_block, preferred_element_t...]
    pallas_call x0 -> x10, Pallas kernels: none -> 141 us  [the longest x2 50.4 us: regroup(): call(kernel, [shape] * plan.groups, 0, 4 * plan.locs * plan.chunk_rows *...]
    dynamic_slice x22 -> x0, local copies, waits for them, and re-layouts: 78.6 us -> none  [the longest x8 54.3 us: step(): lax.dynamic_slice_in_dim(values, first, block, 0)]
    reduce_sum x10 -> x0, other arithmetic: 59.7 us -> none  [the longest x4 49.5 us: step(): total = total * factor + jnp.sum(expo, axis=-1)]
    ppermute x0 -> x33, starting transfers between devices: none -> 51.4 us  [exchange(): lax.ppermute(value, axis, [(i, i ^ step) for i in range(lax.axis_size(axi...]
    slice x5 -> x0, local copies, waits for them, and re-layouts: 49.9 us -> none  [the longest x4 25 us: split_qkv(): return (packed[:, :, 0], packed[:, :, 1], packed[:, :, 2])]
    all_to_all x2 -> x0, blocking collectives: 45.4 us -> none  [the longest x1 24 us: body(): lax.all_to_all(blocked, 'band', split_axis=0, concat_axis=2, tiled=True)[0]]
  transfers between devices with their start and end apart: 2 -> 33, of which waited for: 2 -> 6; matrix products, arithmetic and copies ran while one was open for 2% -> 0% of each run, Pallas kernels for 0% -> 48%
where the time goes in v1:
time: 224 us
  Pallas kernels  141 us (63%)
  starting transfers between devices  51.4 us (23%)
  waiting for transfers between devices  26.1 us (12%)
  local copies, waits for them, and re-layouts  4.88 us (2%)
    ppermute x33, starting transfers between devices, exchange(): lax.ppermute(value, axis, [(i, i ^ step) for i in range(lax.axis_size(axi...  51.4 us
    pallas_call x2, Pallas kernels, regroup(): call(kernel, [shape] * plan.groups, 0, 4 * plan.locs * plan.chunk_rows *...  50.4 us
    pallas_call x2, Pallas kernels, channel(): call(kernel, [jax.ShapeDtypeStruct((bands, locations, width), BF16)] * gr...  38.3 us
    pallas_call x2, Pallas kernels, attend(): call(kernel, [jax.ShapeDtypeStruct((rows, width), BF16)] * plan.locs, 16...  30.6 us
    ppermute x33, waiting for transfers between devices, exchange(): lax.ppermute(value, axis, [(i, i ^ step) for i in range(lax.axis_size(axi...  26.1 us
    pallas_call x2, Pallas kernels, project(): call(kernel, [shape] * 3, 2 * rows * width * 3 * width, 2 * (4 * rows * w...  10.8 us
    pallas_call x1, Pallas kernels, arrange(): call(kernel, [shape] * plan.locs, 2 * plan.loc_dev * tokens.size, 4 * tok...  6.46 us
  transfers between devices with their start and end apart: 33, of which 6 were waited for; matrix products, arithmetic and copies ran while one was open for 0% of the time, Pallas kernels for 48%

profile of v1, /device:TPU:0, one launch (start us, length us, event | category | flops | bytes accessed | tf_op | source)
XLA Modules:
  0.0 223.6 jit_solution(14649211797276778172)
XLA Ops:
  1.3 6.5 %shard_map.100 = (bf16[128,768]{1,0:T(8,128)(2,1)}, bf16[128,768]{1,0:T(8,128)(2,1)}, bf16[128,768]{1,0:T(8,128)(2,1)}, bf16[128,768]{1,0:T(8,128)(2,1)}, bf16[1...) custom-call(s32[8,256]{1,0:T(8,128)} %reshape.35.ids_ref, ...), custom_call_target="tpu_custom_call" | custom-call | flops 402653184 | bytes 3145728 | tf_op jit(solution)/shard_map/pallas_call | solution.py:102
  7.7 5.0 %collective-permute-start.5 = (bf16[128,768]{1,0:T(8,128)(2,1)}, bf16[128,768]{1,0:T(8,128)(2,1)S(1)}, u32[]{:S(2)}, u32[]{:S(2)}) collective-permute-start(bf16[128,768]{1,0:T(8,128)(2,1)} %get-tuple-element.58), channel_id=1, source_target_pairs={{0,6},{1,7},{2,4},{3,5},{4,2},{5,3},{6,0},{7,1},{8,14},{9,15},{10,... | collective-permute-start | bytes 589832 | tf_op jit(solution)/shard_map/ppermute | solution.py:51
  12.9 1.7 collective-permute-start.2
  14.7 3.8 %collective-permute-done.5.rest_0_.rest_12_ = bf16[128,768]{1,0:T(8,128)(2,1)S(1)} collective-permute-done((bf16[128,768]{1,0:T(8,128)(2,1)}, bf16[128,768]{1,0:T(8,128)(2,1)S(1)}, u32[]{:S(2)}, u32[]{:S(2)}) %collective-permute-start.5) | collective-permute-done | bytes 196640 | tf_op jit(solution)/shard_map/ppermute | solution.py:51
  18.5 9.7 %collective-permute-start.3 = (bf16[128,768]{1,0:T(8,128)(2,1)}, bf16[128,768]{1,0:T(8,128)(2,1)S(1)}, u32[]{:S(2)}, u32[]{:S(2)}) collective-permute-start(bf16[128,768]{1,0:T(8,128)(2,1)} %get-tuple-element.55), channel_id=1, source_target_pairs={{0,4},{1,5},{2,6},{3,7},{4,0},{5,1},{6,2},{7,3},{8,12},{9,13},{10,... | collective-permute-start | bytes 589832 | tf_op jit(solution)/shard_map/ppermute | solution.py:51
  28.2 3.9 %collective-permute-start.4 = (bf16[128,768]{1,0:T(8,128)(2,1)}, bf16[128,768]{1,0:T(8,128)(2,1)S(1)}, u32[]{:S(2)}, u32[]{:S(2)}) collective-permute-start(bf16[128,768]{1,0:T(8,128)(2,1)} %get-tuple-element.56), channel_id=1, source_target_pairs={{0,5},{1,4},{2,7},{3,6},{4,1},{5,0},{6,3},{7,2},{8,13},{9,12},{10,... | collective-permute-start | bytes 589832 | tf_op jit(solution)/shard_map/ppermute | solution.py:51
  32.1 4.1 %shard_map.102 = (bf16[256,768]{1,0:T(8,128)(2,1)}, bf16[256,768]{1,0:T(8,128)(2,1)}, bf16[256,768]{1,0:T(8,128)(2,1)}) custom-call(s32[16]{0:T(128)} %index_ref.7, f32[16,768]{1,0:T(8,128)} %table_ref.7, bf16[768,2304]{1,0:T(8,128)(2,1)} %w_ref.5, bf16[128,768]{1,0:T(8,128)(2,1)} %copy-done, bf16[128,768]{1,0:T(8,128)(2,1)} %copy-done.1), custom_call_target="tpu_custom_call" | custom-call | flops 905969664 | bytes 5111808 | tf_op jit(solution)/shard_map/pallas_call | solution.py:139
  36.3 7.0 %collective-permute-done.3.rest_4_.rest_10_ = bf16[128,768]{1,0:T(8,128)(2,1)S(1)} collective-permute-done((bf16[128,768]{1,0:T(8,128)(2,1)}, bf16[128,768]{1,0:T(8,128)(2,1)S(1)}, u32[]{:S(2)}, u32[]{:S(2)}) %collective-permute-start.3) | collective-permute-done | bytes 196640 | tf_op jit(solution)/shard_map/ppermute | solution.py:51
  43.3 2.3 %collective-permute-done.4.rest_5_.rest_11_ = bf16[128,768]{1,0:T(8,128)(2,1)S(1)} collective-permute-done((bf16[128,768]{1,0:T(8,128)(2,1)}, bf16[128,768]{1,0:T(8,128)(2,1)S(1)}, u32[]{:S(2)}, u32[]{:S(2)}) %collective-permute-start.4) | collective-permute-done | bytes 196640 | tf_op jit(solution)/shard_map/ppermute | solution.py:51
  46.3 6.7 %shard_map.101 = (bf16[768,768]{1,0:T(8,128)(2,1)}, bf16[768,768]{1,0:T(8,128)(2,1)}, bf16[768,768]{1,0:T(8,128)(2,1)}) custom-call(s32[16]{0:T(128)} %index_ref.7, f32[16,768]{1,0:T(8,128)} %table_ref.7, bf16[768,2304]{1,0:T(8,128)(2,1)} %w_ref.5, bf16[128,768]{1,0:T(8,128)(2,1)} %get-tuple-element.51.rest_0_.rest_6_, bf16[128,768]{1,0:T(8,128)(2,1)} %copy-done.22, ...), custom_call_target="tpu_custom_call" | custom-call | flops 2717908992 | bytes 8257536 | tf_op jit(solution)/shard_map/pallas_call | solution.py:139
  52.9 15.4 %shard_map.106 = (bf16[64,768]{1,0:T(8,128)(2,1)}, bf16[64,768]{1,0:T(8,128)(2,1)}, bf16[64,768]{1,0:T(8,128)(2,1)}, bf16[64,768]{1,0:T(8,128)(2,1)}, bf16[64,76...) custom-call(s32[16]{0:T(128)} %index_ref.7, f32[16,768]{1,0:T(8,128)} %table_ref.7, ...), custom_call_target="tpu_custom_call" | custom-call | flops 6442450944 | bytes 6684672 | tf_op jit(solution)/shard_map/pallas_call | solution.py:214
  70.6 1.6 collective-permute-start.23
  73.6 2.5 %collective-permute-start.25 = (bf16[64,768]{1,0:T(8,128)(2,1)}, bf16[64,768]{1,0:T(8,128)(2,1)S(1)}, u32[]{:S(2)}, u32[]{:S(2)}) collective-permute-start(bf16[64,768]{1,0:T(8,128)(2,1)} %get-tuple-element.87), channel_id=1, source_target_pairs={{0,6},{1,7},{2,4},{3,5},{4,2},{5,3},{6,0},{7,1},{8,14},{9,15},{10,... | collective-permute-start | bytes 294920 | tf_op jit(solution)/shard_map/ppermute | solution.py:51
  76.8 15.2 %shard_map.103 = (bf16[64,768]{1,0:T(8,128)(2,1)}, bf16[64,768]{1,0:T(8,128)(2,1)}, bf16[64,768]{1,0:T(8,128)(2,1)}, bf16[64,768]{1,0:T(8,128)(2,1)}, bf16[64,76...) custom-call(s32[16]{0:T(128)} %index_ref.7, f32[16,768]{1,0:T(8,128)} %table_ref.7, ...), custom_call_target="tpu_custom_call" | custom-call | flops 6442450944 | bytes 6684672 | tf_op jit(solution)/shard_map/pallas_call | solution.py:214
  92.2 3.1 %collective-permute-start.11 = (bf16[64,768]{1,0:T(8,128)(2,1)}, bf16[64,768]{1,0:T(8,128)(2,1)S(1)}, u32[]{:S(2)}, u32[]{:S(2)}) collective-permute-start(bf16[64,768]{1,0:T(8,128)(2,1)} %get-tuple-element.70), channel_id=1, source_target_pairs={{0,5},{1,4},{2,7},{3,6},{4,1},{5,0},{6,3},{7,2},{8,13},{9,12},{10,... | collective-permute-start | bytes 294920 | tf_op jit(solution)/shard_map/ppermute | solution.py:51
  95.3 2.4 %collective-permute-start.12 = (bf16[64,768]{1,0:T(8,128)(2,1)}, bf16[64,768]{1,0:T(8,128)(2,1)S(1)}, u32[]{:S(2)}, u32[]{:S(2)}) collective-permute-start(bf16[64,768]{1,0:T(8,128)(2,1)} %get-tuple-element.71), channel_id=1, source_target_pairs={{0,6},{1,7},{2,4},{3,5},{4,2},{5,3},{6,0},{7,1},{8,14},{9,15},{10,... | collective-permute-start | bytes 294920 | tf_op jit(solution)/shard_map/ppermute | solution.py:51
  99.2 25.2 %shard_map.107 = (bf16[8,16,768]{2,1,0:T(8,128)(2,1)}, bf16[8,16,768]{2,1,0:T(8,128)(2,1)}, bf16[8,16,768]{2,1,0:T(8,128)(2,1)}, bf16[8,16,768]{2,1,0:T(8,128)(2,1)}) custom-call(bf16[64,768]{1,0:T(8,128)(2,1)} %get-tuple-element.81.refs_0_, bf16[64,768]{1,0:T(8,128)(2,1)} %copy-done.8, bf16[64,768]{1,0:T(8,128)(2,1)} %copy-done.10, ...), custom_call_target="tpu_custom_call" | custom-call | bytes 1572864 | tf_op jit(solution)/shard_map/pallas_call | solution.py:258
  124.5 1.6 collective-permute-start.27
  126.1 1.5 collective-permute-start.28
  129.2 4.6 %collective-permute-done.8.refs_2_ = bf16[64,768]{1,0:T(8,128)(2,1)S(1)} collective-permute-done((bf16[64,768]{1,0:T(8,128)(2,1)}, bf16[64,768]{1,0:T(8,128)(2,1)S(1)}, u32[]{:S(2)}, u32[]{:S(2)}) %collective-permute-start.8) | collective-permute-done | bytes 98336 | tf_op jit(solution)/shard_map/ppermute | solution.py:51
  134.5 25.2 %shard_map.104 = (bf16[8,16,768]{2,1,0:T(8,128)(2,1)}, bf16[8,16,768]{2,1,0:T(8,128)(2,1)}, bf16[8,16,768]{2,1,0:T(8,128)(2,1)}, bf16[8,16,768]{2,1,0:T(8,128)(2,1)}) custom-call(bf16[64,768]{1,0:T(8,128)(2,1)} %get-tuple-element.65.refs_0_, bf16[64,768]{1,0:T(8,128)(2,1)} %copy-done.19, bf16[64,768]{1,0:T(8,128)(2,1)} %copy-done.20, ...), custom_call_target="tpu_custom_call" | custom-call | bytes 1572864 | tf_op jit(solution)/shard_map/pallas_call | solution.py:258
  159.7 1.6 collective-permute-start.14
  161.3 1.5 collective-permute-start.15
  164.0 19.3 %shard_map.108 = (bf16[4,32,768]{2,1,0:T(8,128)(2,1)}, bf16[4,32,768]{2,1,0:T(8,128)(2,1)}, bf16[4,32,768]{2,1,0:T(8,128)(2,1)}, bf16[4,32,768]{2,1,0:T(8,128)(2,1)}) custom-call(bf16[768,2304]{1,0:T(8,128)(2,1)} %qkv_ref.3, bf16[768,768]{1,0:T(8,128)(2,1)} %out_ref.3, bf16[768,3072]{1,0:T(8,128)(2,1)} %up_ref.3, bf16[3072,768]{1,0:T(8,128)(2,1)} %down_ref.3, ...), custom_call_target="tpu_custom_call" | custom-call | flops 7247757312 | bytes 15728640 | tf_op jit(solution)/shard_map/pallas_call | solution.py:306
  183.3 1.5 collective-permute-start.30
  184.9 1.5 collective-permute-start.31
  187.6 19.0 %shard_map.105 = (bf16[4,32,768]{2,1,0:T(8,128)(2,1)}, bf16[4,32,768]{2,1,0:T(8,128)(2,1)}, bf16[4,32,768]{2,1,0:T(8,128)(2,1)}, bf16[4,32,768]{2,1,0:T(8,128)(2,1)}) custom-call(bf16[768,2304]{1,0:T(8,128)(2,1)} %qkv_ref.3, bf16[768,768]{1,0:T(8,128)(2,1)} %out_ref.3, bf16[768,3072]{1,0:T(8,128)(2,1)} %up_ref.3, bf16[3072,768]{1,0:T(8,128)(2,1)} %down_ref.3, ...), custom_call_target="tpu_custom_call" | custom-call | flops 7247757312 | bytes 15728640 | tf_op jit(solution)/shard_map/pallas_call | solution.py:306
  206.6 1.5 collective-permute-start.17
  208.1 1.5 collective-permute-start.18
  210.2 4.5 %collective-permute-done.17.refs_1_ = bf16[4,32,768]{2,1,0:T(8,128)(2,1)S(1)} collective-permute-done((bf16[4,32,768]{2,1,0:T(8,128)(2,1)}, bf16[4,32,768]{2,1,0:T(8,128)(2,1)S(1)}, u32[]{:S(2)}, u32[]{:S(2)}) %collective-permute-start.17) | collective-permute-done | bytes 196640 | tf_op jit(solution)/shard_map/ppermute | solution.py:51
  214.7 3.8 %collective-permute-done.18.refs_2_ = bf16[4,32,768]{2,1,0:T(8,128)(2,1)S(1)} collective-permute-done((bf16[4,32,768]{2,1,0:T(8,128)(2,1)}, bf16[4,32,768]{2,1,0:T(8,128)(2,1)S(1)}, u32[]{:S(2)}, u32[]{:S(2)}) %collective-permute-start.18) | collective-permute-done | bytes 196640 | tf_op jit(solution)/shard_map/ppermute | solution.py:51
  219.3 4.3 %shard_map.109 = bf16[256,4,768]{2,1,0:T(4,128)(2,1)} custom-call(s32[8,256]{1,0:T(8,128)} %reshape.35.ids_ref, bf16[4,32,768]{2,1,0:T(8,128)(2,1)} %get-tuple-element.77.refs_0_, bf16[4,32,768]{2,1,0:T(8,128)(2,1)} %copy-done.5, bf16[4,32,768]{2,1,0:T(8,128)(2,1)} %copy-done.6, bf16[4,32,768]{2,1,0:T(8,128)(2,1)} %copy-done.7, ...), custom_call_target="tpu_custom_call" | custom-call | flops 402653184 | bytes 3145728 | tf_op jit(solution)/shard_map/pallas_call | solution.py:348
  (111 shorter events, 14.2 us)
Async XLA Ops:
  7.7 10.7 %collective-permute-start.5 = (bf16[128,768]{1,0:T(8,128)(2,1)}, bf16[128,768]{1,0:T(8,128)(2,1)S(1)}, u32[]{:S(2)}, u32[]{:S(2)}) collective-permute-start(bf16[128,768]{1,0:T(8,128)(2,1)} %get-tuple-element.58), channel_id=1, source_target_pairs={{0,6},{1,7},{2,4},{3,5},{4,2},{5,3},{6,0},{7,1},{8,14},{9,15},{10,... | collective-permute-start | bytes 589832 | tf_op jit(solution)/shard_map/ppermute | solution.py:51
  12.8 15.4 %collective-permute-start.6 = (bf16[128,768]{1,0:T(8,128)(2,1)}, bf16[128,768]{1,0:T(8,128)(2,1)S(1)}, u32[]{:S(2)}, u32[]{:S(2)}) collective-permute-start(bf16[128,768]{1,0:T(8,128)(2,1)} %get-tuple-element.59), channel_id=1, source_target_pairs={{0,7},{1,6},{2,5},{3,4},{4,3},{5,2},{6,1},{7,0},{8,15},{9,14},{10,... | collective-permute-start | bytes 589832 | tf_op jit(solution)/shard_map/ppermute | solution.py:51
  12.8 23.5 %collective-permute-start = (bf16[128,768]{1,0:T(8,128)(2,1)}, bf16[128,768]{1,0:T(8,128)(2,1)S(1)}, u32[]{:S(2)}, u32[]{:S(2)}) collective-permute-start(bf16[128,768]{1,0:T(8,128)(2,1)} %get-tuple-element.52), channel_id=1, source_target_pairs={{0,1},{1,0},{2,3},{3,2},{4,5},{5,4},{6,7},{7,6},{8,9},{9,8},{10,11... | collective-permute-start | bytes 589832 | tf_op jit(solution)/shard_map/ppermute | solution.py:51
  12.9 23.3 %collective-permute-start.1 = (bf16[128,768]{1,0:T(8,128)(2,1)}, bf16[128,768]{1,0:T(8,128)(2,1)S(1)}, u32[]{:S(2)}, u32[]{:S(2)}) collective-permute-start(bf16[128,768]{1,0:T(8,128)(2,1)} %get-tuple-element.53), channel_id=1, source_target_pairs={{0,2},{1,3},{2,0},{3,1},{4,6},{5,7},{6,4},{7,5},{8,10},{9,11},{10,... | collective-permute-start | bytes 589832 | tf_op jit(solution)/shard_map/ppermute | solution.py:51
  12.9 23.3 %collective-permute-start.2 = (bf16[128,768]{1,0:T(8,128)(2,1)}, bf16[128,768]{1,0:T(8,128)(2,1)S(1)}, u32[]{:S(2)}, u32[]{:S(2)}) collective-permute-start(bf16[128,768]{1,0:T(8,128)(2,1)} %get-tuple-element.54), channel_id=1, source_target_pairs={{0,3},{1,2},{2,1},{3,0},{4,7},{5,6},{6,5},{7,4},{8,11},{9,10},{10,... | collective-permute-start | bytes 589832 | tf_op jit(solution)/shard_map/ppermute | solution.py:51
  18.5 24.8 %collective-permute-start.3 = (bf16[128,768]{1,0:T(8,128)(2,1)}, bf16[128,768]{1,0:T(8,128)(2,1)S(1)}, u32[]{:S(2)}, u32[]{:S(2)}) collective-permute-start(bf16[128,768]{1,0:T(8,128)(2,1)} %get-tuple-element.55), channel_id=1, source_target_pairs={{0,4},{1,5},{2,6},{3,7},{4,0},{5,1},{6,2},{7,3},{8,12},{9,13},{10,... | collective-permute-start | bytes 589832 | tf_op jit(solution)/shard_map/ppermute | solution.py:51
  28.2 17.4 %collective-permute-start.4 = (bf16[128,768]{1,0:T(8,128)(2,1)}, bf16[128,768]{1,0:T(8,128)(2,1)S(1)}, u32[]{:S(2)}, u32[]{:S(2)}) collective-permute-start(bf16[128,768]{1,0:T(8,128)(2,1)} %get-tuple-element.56), channel_id=1, source_target_pairs={{0,5},{1,4},{2,7},{3,6},{4,1},{5,0},{6,3},{7,2},{8,13},{9,12},{10,... | collective-permute-start | bytes 589832 | tf_op jit(solution)/shard_map/ppermute | solution.py:51
  69.2 6.9 %collective-permute-start.21 = (bf16[64,768]{1,0:T(8,128)(2,1)}, bf16[64,768]{1,0:T(8,128)(2,1)S(1)}, u32[]{:S(2)}, u32[]{:S(2)}) collective-permute-start(bf16[64,768]{1,0:T(8,128)(2,1)} %get-tuple-element.83), channel_id=1, source_target_pairs={{0,2},{1,3},{2,0},{3,1},{4,6},{5,7},{6,4},{7,5},{8,10},{9,11},{10,... | collective-permute-start | bytes 294920 | tf_op jit(solution)/shard_map/ppermute | solution.py:51
  69.2 22.8 %collective-permute-start.22 = (bf16[64,768]{1,0:T(8,128)(2,1)}, bf16[64,768]{1,0:T(8,128)(2,1)S(1)}, u32[]{:S(2)}, u32[]{:S(2)}) collective-permute-start(bf16[64,768]{1,0:T(8,128)(2,1)} %get-tuple-element.84), channel_id=1, source_target_pairs={{0,3},{1,2},{2,1},{3,0},{4,7},{5,6},{6,5},{7,4},{8,11},{9,10},{10,... | collective-permute-start | bytes 294920 | tf_op jit(solution)/shard_map/ppermute | solution.py:51
  70.6 21.5 %collective-permute-start.23 = (bf16[64,768]{1,0:T(8,128)(2,1)}, bf16[64,768]{1,0:T(8,128)(2,1)S(1)}, u32[]{:S(2)}, u32[]{:S(2)}) collective-permute-start(bf16[64,768]{1,0:T(8,128)(2,1)} %get-tuple-element.85), channel_id=1, source_target_pairs={{0,4},{1,5},{2,6},{3,7},{4,0},{5,1},{6,2},{7,3},{8,12},{9,13},{10,... | collective-permute-start | bytes 294920 | tf_op jit(solution)/shard_map/ppermute | solution.py:51
  72.3 23.0 %collective-permute-start.24 = (bf16[64,768]{1,0:T(8,128)(2,1)}, bf16[64,768]{1,0:T(8,128)(2,1)S(1)}, u32[]{:S(2)}, u32[]{:S(2)}) collective-permute-start(bf16[64,768]{1,0:T(8,128)(2,1)} %get-tuple-element.86), channel_id=1, source_target_pairs={{0,5},{1,4},{2,7},{3,6},{4,1},{5,0},{6,3},{7,2},{8,13},{9,12},{10,... | collective-permute-start | bytes 294920 | tf_op jit(solution)/shard_map/ppermute | solution.py:51
  73.6 24.0 %collective-permute-start.25 = (bf16[64,768]{1,0:T(8,128)(2,1)}, bf16[64,768]{1,0:T(8,128)(2,1)S(1)}, u32[]{:S(2)}, u32[]{:S(2)}) collective-permute-start(bf16[64,768]{1,0:T(8,128)(2,1)} %get-tuple-element.87), channel_id=1, source_target_pairs={{0,6},{1,7},{2,4},{3,5},{4,2},{5,3},{6,0},{7,1},{8,14},{9,15},{10,... | collective-permute-start | bytes 294920 | tf_op jit(solution)/shard_map/ppermute | solution.py:51
  76.1 22.3 %collective-permute-start.26 = (bf16[64,768]{1,0:T(8,128)(2,1)}, bf16[64,768]{1,0:T(8,128)(2,1)S(1)}, u32[]{:S(2)}, u32[]{:S(2)}) collective-permute-start(bf16[64,768]{1,0:T(8,128)(2,1)} %get-tuple-element.88), channel_id=1, source_target_pairs={{0,7},{1,6},{2,5},{3,4},{4,3},{5,2},{6,1},{7,0},{8,15},{9,14},{10,... | collective-permute-start | bytes 294920 | tf_op jit(solution)/shard_map/ppermute | solution.py:51
  92.1 32.4 %collective-permute-start.10 = (bf16[64,768]{1,0:T(8,128)(2,1)}, bf16[64,768]{1,0:T(8,128)(2,1)S(1)}, u32[]{:S(2)}, u32[]{:S(2)}) collective-permute-start(bf16[64,768]{1,0:T(8,128)(2,1)} %get-tuple-element.69), channel_id=1, source_target_pairs={{0,4},{1,5},{2,6},{3,7},{4,0},{5,1},{6,2},{7,3},{8,12},{9,13},{10,... | collective-permute-start | bytes 294920 | tf_op jit(solution)/shard_map/ppermute | solution.py:51
  92.2 33.8 %collective-permute-start.11 = (bf16[64,768]{1,0:T(8,128)(2,1)}, bf16[64,768]{1,0:T(8,128)(2,1)S(1)}, u32[]{:S(2)}, u32[]{:S(2)}) collective-permute-start(bf16[64,768]{1,0:T(8,128)(2,1)} %get-tuple-element.70), channel_id=1, source_target_pairs={{0,5},{1,4},{2,7},{3,6},{4,1},{5,0},{6,3},{7,2},{8,13},{9,12},{10,... | collective-permute-start | bytes 294920 | tf_op jit(solution)/shard_map/ppermute | solution.py:51
  95.3 32.3 %collective-permute-start.12 = (bf16[64,768]{1,0:T(8,128)(2,1)}, bf16[64,768]{1,0:T(8,128)(2,1)S(1)}, u32[]{:S(2)}, u32[]{:S(2)}) collective-permute-start(bf16[64,768]{1,0:T(8,128)(2,1)} %get-tuple-element.71), channel_id=1, source_target_pairs={{0,6},{1,7},{2,4},{3,5},{4,2},{5,3},{6,0},{7,1},{8,14},{9,15},{10,... | collective-permute-start | bytes 294920 | tf_op jit(solution)/shard_map/ppermute | solution.py:51
  97.6 30.4 %collective-permute-start.13 = (bf16[64,768]{1,0:T(8,128)(2,1)}, bf16[64,768]{1,0:T(8,128)(2,1)S(1)}, u32[]{:S(2)}, u32[]{:S(2)}) collective-permute-start(bf16[64,768]{1,0:T(8,128)(2,1)} %get-tuple-element.72), channel_id=1, source_target_pairs={{0,7},{1,6},{2,5},{3,4},{4,3},{5,2},{6,1},{7,0},{8,15},{9,14},{10,... | collective-permute-start | bytes 294920 | tf_op jit(solution)/shard_map/ppermute | solution.py:51
  98.4 29.7 %collective-permute-start.7 = (bf16[64,768]{1,0:T(8,128)(2,1)}, bf16[64,768]{1,0:T(8,128)(2,1)S(1)}, u32[]{:S(2)}, u32[]{:S(2)}) collective-permute-start(bf16[64,768]{1,0:T(8,128)(2,1)} %get-tuple-element.66), channel_id=1, source_target_pairs={{0,1},{1,0},{2,3},{3,2},{4,5},{5,4},{6,7},{7,6},{8,9},{9,8},{10,11... | collective-permute-start | bytes 294920 | tf_op jit(solution)/shard_map/ppermute | solution.py:51
  124.5 38.3 %collective-permute-start.27 = (bf16[8,16,768]{2,1,0:T(8,128)(2,1)}, bf16[8,16,768]{2,1,0:T(8,128)(2,1)S(1)}, u32[]{:S(2)}, u32[]{:S(2)}) collective-permute-start(bf16[8,16,768]{2,1,0:T(8,128)(2,1)} %get-tuple-element.90), channel_id=1, source_target_pairs={{0,8},{8,0},{16,24},{24,16},{1,9},{9,1},{17,25},{25,17},{2,10},{10... | collective-permute-start | bytes 589832 | tf_op jit(solution)/shard_map/ppermute | solution.py:51
  126.1 37.2 %collective-permute-start.28 = (bf16[8,16,768]{2,1,0:T(8,128)(2,1)}, bf16[8,16,768]{2,1,0:T(8,128)(2,1)S(1)}, u32[]{:S(2)}, u32[]{:S(2)}) collective-permute-start(bf16[8,16,768]{2,1,0:T(8,128)(2,1)} %get-tuple-element.91), channel_id=1, source_target_pairs={{0,16},{8,24},{16,0},{24,8},{1,17},{9,25},{17,1},{25,9},{2,18},{10... | collective-permute-start | bytes 589832 | tf_op jit(solution)/shard_map/ppermute | solution.py:51
  127.6 35.7 %collective-permute-start.29 = (bf16[8,16,768]{2,1,0:T(8,128)(2,1)}, bf16[8,16,768]{2,1,0:T(8,128)(2,1)S(1)}, u32[]{:S(2)}, u32[]{:S(2)}) collective-permute-start(bf16[8,16,768]{2,1,0:T(8,128)(2,1)} %get-tuple-element.92), channel_id=1, source_target_pairs={{0,24},{8,16},{16,8},{24,0},{1,25},{9,17},{17,9},{25,1},{2,26},{10... | collective-permute-start | bytes 589832 | tf_op jit(solution)/shard_map/ppermute | solution.py:51
  128.1 5.7 %collective-permute-start.8 = (bf16[64,768]{1,0:T(8,128)(2,1)}, bf16[64,768]{1,0:T(8,128)(2,1)S(1)}, u32[]{:S(2)}, u32[]{:S(2)}) collective-permute-start(bf16[64,768]{1,0:T(8,128)(2,1)} %get-tuple-element.67), channel_id=1, source_target_pairs={{0,2},{1,3},{2,0},{3,1},{4,6},{5,7},{6,4},{7,5},{8,10},{9,11},{10,... | collective-permute-start | bytes 294920 | tf_op jit(solution)/shard_map/ppermute | solution.py:51
  128.1 5.7 %collective-permute-start.9 = (bf16[64,768]{1,0:T(8,128)(2,1)}, bf16[64,768]{1,0:T(8,128)(2,1)S(1)}, u32[]{:S(2)}, u32[]{:S(2)}) collective-permute-start(bf16[64,768]{1,0:T(8,128)(2,1)} %get-tuple-element.68), channel_id=1, source_target_pairs={{0,3},{1,2},{2,1},{3,0},{4,7},{5,6},{6,5},{7,4},{8,11},{9,10},{10,... | collective-permute-start | bytes 294920 | tf_op jit(solution)/shard_map/ppermute | solution.py:51
  159.7 26.7 %collective-permute-start.14 = (bf16[8,16,768]{2,1,0:T(8,128)(2,1)}, bf16[8,16,768]{2,1,0:T(8,128)(2,1)S(1)}, u32[]{:S(2)}, u32[]{:S(2)}) collective-permute-start(bf16[8,16,768]{2,1,0:T(8,128)(2,1)} %get-tuple-element.74), channel_id=1, source_target_pairs={{0,8},{8,0},{16,24},{24,16},{1,9},{9,1},{17,25},{25,17},{2,10},{10... | collective-permute-start | bytes 589832 | tf_op jit(solution)/shard_map/ppermute | solution.py:51
  161.3 25.6 %collective-permute-start.15 = (bf16[8,16,768]{2,1,0:T(8,128)(2,1)}, bf16[8,16,768]{2,1,0:T(8,128)(2,1)S(1)}, u32[]{:S(2)}, u32[]{:S(2)}) collective-permute-start(bf16[8,16,768]{2,1,0:T(8,128)(2,1)} %get-tuple-element.75), channel_id=1, source_target_pairs={{0,16},{8,24},{16,0},{24,8},{1,17},{9,25},{17,1},{25,9},{2,18},{10... | collective-permute-start | bytes 589832 | tf_op jit(solution)/shard_map/ppermute | solution.py:51
  162.8 24.1 %collective-permute-start.16 = (bf16[8,16,768]{2,1,0:T(8,128)(2,1)}, bf16[8,16,768]{2,1,0:T(8,128)(2,1)S(1)}, u32[]{:S(2)}, u32[]{:S(2)}) collective-permute-start(bf16[8,16,768]{2,1,0:T(8,128)(2,1)} %get-tuple-element.76), channel_id=1, source_target_pairs={{0,24},{8,16},{16,8},{24,0},{1,25},{9,17},{17,9},{25,1},{2,26},{10... | collective-permute-start | bytes 589832 | tf_op jit(solution)/shard_map/ppermute | solution.py:51
  183.3 26.3 %collective-permute-start.30 = (bf16[4,32,768]{2,1,0:T(8,128)(2,1)}, bf16[4,32,768]{2,1,0:T(8,128)(2,1)S(1)}, u32[]{:S(2)}, u32[]{:S(2)}) collective-permute-start(bf16[4,32,768]{2,1,0:T(8,128)(2,1)} %get-tuple-element.94), channel_id=1, source_target_pairs={{0,8},{8,0},{16,24},{24,16},{1,9},{9,1},{17,25},{25,17},{2,10},{10... | collective-permute-start | bytes 589832 | tf_op jit(solution)/shard_map/ppermute | solution.py:51
  184.9 25.3 %collective-permute-start.31 = (bf16[4,32,768]{2,1,0:T(8,128)(2,1)}, bf16[4,32,768]{2,1,0:T(8,128)(2,1)S(1)}, u32[]{:S(2)}, u32[]{:S(2)}) collective-permute-start(bf16[4,32,768]{2,1,0:T(8,128)(2,1)} %get-tuple-element.95), channel_id=1, source_target_pairs={{0,16},{8,24},{16,0},{24,8},{1,17},{9,25},{17,1},{25,9},{2,18},{10... | collective-permute-start | bytes 589832 | tf_op jit(solution)/shard_map/ppermute | solution.py:51
  186.4 23.8 %collective-permute-start.32 = (bf16[4,32,768]{2,1,0:T(8,128)(2,1)}, bf16[4,32,768]{2,1,0:T(8,128)(2,1)S(1)}, u32[]{:S(2)}, u32[]{:S(2)}) collective-permute-start(bf16[4,32,768]{2,1,0:T(8,128)(2,1)} %get-tuple-element.96), channel_id=1, source_target_pairs={{0,24},{8,16},{16,8},{24,0},{1,25},{9,17},{17,9},{25,1},{2,26},{10... | collective-permute-start | bytes 589832 | tf_op jit(solution)/shard_map/ppermute | solution.py:51
  206.6 8.1 %collective-permute-start.17 = (bf16[4,32,768]{2,1,0:T(8,128)(2,1)}, bf16[4,32,768]{2,1,0:T(8,128)(2,1)S(1)}, u32[]{:S(2)}, u32[]{:S(2)}) collective-permute-start(bf16[4,32,768]{2,1,0:T(8,128)(2,1)} %get-tuple-element.78), channel_id=1, source_target_pairs={{0,8},{8,0},{16,24},{24,16},{1,9},{9,1},{17,25},{25,17},{2,10},{10... | collective-permute-start | bytes 589832 | tf_op jit(solution)/shard_map/ppermute | solution.py:51
  208.1 10.4 %collective-permute-start.18 = (bf16[4,32,768]{2,1,0:T(8,128)(2,1)}, bf16[4,32,768]{2,1,0:T(8,128)(2,1)S(1)}, u32[]{:S(2)}, u32[]{:S(2)}) collective-permute-start(bf16[4,32,768]{2,1,0:T(8,128)(2,1)} %get-tuple-element.79), channel_id=1, source_target_pairs={{0,16},{8,24},{16,0},{24,8},{1,17},{9,25},{17,1},{25,9},{2,18},{10... | collective-permute-start | bytes 589832 | tf_op jit(solution)/shard_map/ppermute | solution.py:51
  209.7 8.9 %collective-permute-start.19 = (bf16[4,32,768]{2,1,0:T(8,128)(2,1)}, bf16[4,32,768]{2,1,0:T(8,128)(2,1)S(1)}, u32[]{:S(2)}, u32[]{:S(2)}) collective-permute-start(bf16[4,32,768]{2,1,0:T(8,128)(2,1)} %get-tuple-element.80), channel_id=1, source_target_pairs={{0,24},{8,16},{16,8},{24,0},{1,25},{9,17},{17,9},{25,1},{2,26},{10... | collective-permute-start | bytes 589832 | tf_op jit(solution)/shard_map/ppermute | solution.py:51
  (34 other events, 180.1 us)
